TPU v7x, 256 devices: a whole 4x4x8 slice. The times are simulated.
256 devices in a mesh: serve: 16 (over z, core), tensor: 16 (over y, x).
Axes of the slice: x: 4, y: 4, z: 8, core: 2. Of those that a mesh axis runs over, the one named last changes fastest.
Arguments:
- hidden: bfloat16 [1024, 8192], P('serve', 'tensor'), may hold values from -6 to 6
- query_weight: bfloat16 [8192, 4096], P(None, 'tensor'), may hold values from -0.0625 to 0.0625
- adapter_down: bfloat16 [128, 8192, 64], P('serve', 'tensor'), may hold values from -0.0625 to 0.0625
- adapter_up: bfloat16 [128, 64, 4096], P('serve', None, 'tensor'), may hold values from -0.75 to 0.75
- rotated_key_cache: bfloat16 [1024, 4, 512, 128], P(('serve', 'tensor')), may hold values from -900 to 900
- cached_value_rows: bfloat16 [1024, 4, 512, 128], P(('serve', 'tensor')), may hold values from -24 to 24
- cached_length: int32 [1024], P('serve'), may hold values from 1 to 512, as said below
- request_adapter: int32 [1024], P('serve'), may hold values from 0 to 127, as said below
- group_adapters: int32 [16, 16], replicated, may hold values from -1 to 127, as said below
- adapter_pool_row: int32 [128], replicated, may hold values from 0 to 127, as said below
Outputs:
- attention: bfloat16 [1024, 4096], P(('serve', 'tensor'))
Inputs may be any that keep to these rules, and one draw needn't show every extreme that they name: `request_adapter`: each request's id is a non-negative entry of its group's row of group_adapters (group = request // 64). `group_adapters`: the ids of a group are distinct; its live entries come first, then -1 entries; a group has 2 or more live entries, and some group has no -1 entry; every live entry is used by some request of the group; in every group at most 2 live ids have the same adapter_pool_row[id] // 8, and some group has exactly 2 with one such value in every draw. A permutation: adapter a is stored at row adapter_pool_row[a] of adapter_down and adapter_up. `cached_length`: some request has 512 cached positions.
All inputs are finite; a program needn't handle non-finite values.
Results may differ from a plain program's by a relative error of at most 0.02.
Values may be sent and summed in bfloat16 or wider, within the bound.
No kernel may reach another device: no remote copies, remote signals or barrier semaphores. Data moves between devices by JAX's collectives and lax.ppermute only.
A program may use at most 64 MiB of HBM per device.

v0:
```python
import math

import jax
import jax.numpy as jnp
from jax import lax
from jax.sharding import PartitionSpec as P

ADAPTER_SCALE = 0.5
ROPE_BASE = 500000.0
NEG_LARGE = -1e30


def rotate_query(query_heads, positions):
    half_width = query_heads.shape[-1] // 2
    exponent = jnp.arange(half_width, dtype=jnp.float32) * (2.0 / query_heads.shape[-1])
    inverse = jnp.exp(-math.log(ROPE_BASE) * exponent)
    angles = positions.astype(jnp.float32)[:, None] * inverse[None, :]
    cosine = jnp.cos(angles)[:, None, :]
    sine_part = jnp.sin(angles)[:, None, :]
    first_half = query_heads[..., :half_width]
    second_half = query_heads[..., half_width:]
    return jnp.concatenate(
        [
            first_half * cosine - second_half * sine_part,
            second_half * cosine + first_half * sine_part,
        ],
        axis=-1,
    )


def attend_rows(row_query, rotated_key_cache, cached_value_rows, lengths):
    local_rows, kv_heads, cache_count, head_dim = rotated_key_cache.shape
    grouped = row_query.reshape(local_rows, kv_heads, -1, head_dim)
    scores = jnp.einsum(
        "rkgd,rktd->rkgt", grouped, rotated_key_cache, preferred_element_type=jnp.float32
    ) * head_dim ** (-0.5)
    valid_mask = (jnp.arange(cache_count)[None, :] < lengths[:, None])[:, None, None, :]
    row_max = jnp.max(jnp.where(valid_mask, scores, NEG_LARGE), axis=3, keepdims=True)
    weights = jnp.where(valid_mask, jnp.exp(scores - row_max), 0.0).astype(jnp.bfloat16)
    totals = jnp.sum(weights.astype(jnp.float32), axis=3)
    numerator = jnp.einsum(
        "rkgt,rktd->rkgd", weights, cached_value_rows, preferred_element_type=jnp.float32
    )
    return (numerator / totals[..., None]).reshape(local_rows, -1).astype(jnp.bfloat16)


def sum_shrink(partial_pick):
    return lax.psum(partial_pick, "tensor").astype(jnp.bfloat16)


def on_device(
    hidden,
    query_weight,
    adapter_down,
    adapter_up,
    rotated_key_cache,
    cached_value_rows,
    cached_length,
    request_adapter,
    group_adapters,
    adapter_pool_row,
):
    group_index = lax.axis_index("serve")
    tensor_index = lax.axis_index("tensor")
    row_count = hidden.shape[0]
    slot_count = group_adapters.shape[1]
    rank_columns = adapter_down.shape[2]
    query_columns = adapter_up.shape[2]
    head_dim = rotated_key_cache.shape[3]
    local_rows = rotated_key_cache.shape[0]
    all_pool = jnp.take(adapter_pool_row, jnp.maximum(group_adapters, 0), axis=0)
    my_list = lax.dynamic_index_in_dim(group_adapters, group_index, 0, keepdims=False)
    my_pool = lax.dynamic_index_in_dim(all_pool, group_index, 0, keepdims=False)
    my_live = my_list >= 0
    pieces = (
        lax.all_gather(adapter_down, "serve", axis=0, tiled=True),
        lax.all_gather(adapter_up, "serve", axis=0, tiled=True),
    )
    count = pieces[0].shape[0]
    positions = jnp.arange(count, dtype=jnp.int32)
    chosen = ((my_pool[:, None] == positions[None, :]) & my_live[:, None]).astype(jnp.bfloat16)
    down_pick = jnp.einsum("sa,adk->sdk", chosen, pieces[0], preferred_element_type=jnp.float32)
    up_pick = jnp.einsum("sa,akq->skq", chosen, pieces[1], preferred_element_type=jnp.float32)
    fetched_down = down_pick.astype(jnp.bfloat16)
    fetched_up = up_pick.astype(jnp.bfloat16)
    row_slot = (request_adapter[:, None] == my_list[None, :]) & my_live[None, :]
    partial_value = jnp.einsum(
        "rd,sdk->rsk", hidden, fetched_down, preferred_element_type=jnp.float32
    )
    partial_pick = jnp.sum(jnp.where(row_slot[:, :, None], partial_value, 0.0), axis=1)
    shrunk = sum_shrink(partial_pick)
    wide_shrunk = jnp.where(
        row_slot[:, :, None], shrunk[:, None, :], jnp.zeros((), jnp.bfloat16)
    ).reshape(row_count, slot_count * rank_columns)
    widen_back = jnp.dot(
        wide_shrunk,
        fetched_up.reshape(slot_count * rank_columns, query_columns),
        preferred_element_type=jnp.float32,
    )
    base_product = jnp.dot(
        lax.all_gather(hidden, "tensor", axis=1, tiled=True),
        query_weight,
        preferred_element_type=jnp.float32,
    )
    query_linear = base_product + ADAPTER_SCALE * widen_back
    query_rows = (
        rotate_query(
            query_linear.reshape(row_count, query_columns // head_dim, head_dim), cached_length
        )
        .reshape(row_count, query_columns)
        .astype(jnp.bfloat16)
    )
    row_query = lax.all_to_all(query_rows, "tensor", split_axis=0, concat_axis=1, tiled=True)
    lengths = lax.dynamic_slice_in_dim(cached_length, tensor_index * local_rows, local_rows, 0)
    return attend_rows(row_query, rotated_key_cache, cached_value_rows, lengths)


def solution(mesh):
    placed = (
        P("serve", "tensor"),
        P(None, "tensor"),
        P("serve", "tensor", None),
        P("serve", None, "tensor"),
        P(("serve", "tensor"), None, None, None),
        P(("serve", "tensor"), None, None, None),
        P("serve"),
        P("serve"),
        P(),
        P(),
    )
    return jax.shard_map(
        on_device,
        mesh=mesh,
        in_specs=placed,
        out_specs=P(("serve", "tensor"), None),
        check_vma=False,
    )
```

profile of v0, /device:TPU:2, one launch (start us, length us, event | category | flops | bytes accessed | tf_op | source)
XLA Modules:
  0.0 270.3 jit_solution(11626045351630970376)
XLA Ops:
  6.5 0.7 all-gather.4.cloned.1.call-update
  7.3 0.7 all-gather.8.cloned.1.call-update
  8.0 0.0 all-gather.6.cloned.1.call-start
  8.1 0.7 all-gather.6.cloned.1.call-update
  8.8 0.7 broadcast_maximum_fusion
  9.5 0.1 reshape.146
  9.6 1.9 gather_fusion
  11.4 0.1 reshape.145
  11.5 0.1 dynamic_slice.10
  11.6 0.7 compare_bitcast_fusion
  12.3 0.7 broadcast_compare_fusion
  13.0 0.1 compare_and_fusion
  13.1 0.2 multiply_cosine_fusion
  13.3 47.5 %all-gather.4.cloned.1.call-done = bf16[64,8192]{1,0:T(8,128)(2,1)} async-done(((bf16[64,512]{1,0:T(8,128)(2,1)}), bf16[64,8192]{1,0:T(8,128)(2,1)}) %all-gather.4.cloned.1.call-update) | async-done | bytes 1048592 | tf_op jit(solution)/shard_map/all_gather | solution.py:101
  60.8 3.3 %fusion.44 = f32[64,256]{1,0:T(8,128)S(1)} fusion(bf16[64,8192]{1,0:T(8,128)(2,1)} %all-gather.4.cloned.1.call-done, bf16[8192,256]{1,0:T(8,128)(2,1)} %param.11), kind=kOutput, calls=%fused_computation.62 | convolution fusion | flops 268435456 | bytes 5308416 | tf_op jit(solution)/shard_map/dot_general | solution.py:100
  64.1 40.4 %all-gather.8.cloned.1.call-done = bf16[128,64,256]{2,1,0:T(8,128)(2,1)} async-done(((bf16[8,64,256]{2,1,0:T(8,128)(2,1)}), bf16[128,64,256]{2,1,0:T(8,128)(2,1)}) %all-gather.8.cloned.1.call-update) | async-done | bytes 4194320 | tf_op jit(solution)/shard_map/all_gather | solution.py:77
  104.5 4.5 %fusion.8 = bf16[16,64,256]{2,0,1:T(8,128)(2,1)S(1)} fusion(bf16[128,64,256]{2,1,0:T(8,128)(2,1)} %all-gather.8.cloned.1.call-done, s32[16]{0:T(128)S(1)} %fusion.39, pred[16]{0:T(512)(128)(4,1)S(1)} %get-tuple-element.5), kind=kOutput, calls=%fused_computation.7 | convolution fusion | flops 67375104 | bytes 4718672 | tf_op jit(solution)/shard_map/sa,akq->skq/dot_general | solution.py:83
  109.0 51.8 %all-gather.6.cloned.1.call-done = bf16[128,512,64]{1,2,0:T(8,128)(2,1)} async-done(((bf16[8,512,64]{1,2,0:T(8,128)(2,1)}), bf16[128,512,64]{1,2,0:T(8,128)(2,1)}) %all-gather.6.cloned.1.call-update) | async-done | bytes 8388624 | tf_op jit(solution)/shard_map/all_gather | solution.py:76
  160.9 12.4 %fusion.5 = bf16[16,512,64]{1,0,2:T(8,128)(2,1)S(1)} fusion(bf16[128,512,64]{1,2,0:T(8,128)(2,1)} %all-gather.6.cloned.1.call-done, s32[16]{0:T(128)S(1)} %fusion.39, pred[16]{0:T(512)(128)(4,1)S(1)} %get-tuple-element.5), kind=kOutput, calls=%fused_computation.6 | convolution fusion | flops 134746112 | bytes 9437264 | tf_op jit(solution)/shard_map/sa,adk->sdk/dot_general | solution.py:82
  173.3 1.2 fusion.12
  174.5 69.3 %psum.7 = bf16[64,64]{0,1:T(8,128)(2,1)S(1)} all-reduce(f32[64,64]{0,1:T(8,128)S(1)} %fusion.12), channel_id=1, replica_groups=mesh['serve'=16,'tensor'=16] {'tensor'}, use_global_device_ids=true, to_apply=%region_1.2 | all-reduce | flops 4096 | bytes 24576 | tf_op jit(solution)/shard_map/psum | solution.py:48
  243.8 0.3 fusion.18
  244.1 0.2 subtract_convert_fusion
  244.3 0.1 pad_maximum_fusion
  244.4 0.6 convert_element_type.34
  245.1 8.9 %all-to-all-start = ((bf16[16,4,256]{2,1,0:T(4,128)(2,1)}), bf16[16,4,256]{2,1,0:T(4,128)(2,1)S(1)}, u32[]{:S(2)}, u32[]{:S(2)}) async-start(bf16[16,4,256]{2,1,0:T(4,128)(2,1)} %convert_element_type.34), calls=%async_computation | async-start | bytes 65536 | tf_op jit(solution)/shard_map/all_to_all | solution.py:113
  253.9 0.1 iota_compare_fusion.1
  254.0 6.2 %all-to-all-done = bf16[16,4,256]{2,1,0:T(4,128)(2,1)S(1)} async-done(((bf16[16,4,256]{2,1,0:T(4,128)(2,1)}), bf16[16,4,256]{2,1,0:T(4,128)(2,1)S(1)}, u32[]{:S(2)}, u32[]{:S(2)}) %all-to-all-start) | async-done | bytes 32800 | tf_op jit(solution)/shard_map/all_to_all | solution.py:113
  260.3 0.6 convolution_multiply_fusion
  260.9 0.2 convert_reduce_fusion
  261.2 2.0 fusion.20
  263.1 0.7 copy.34
  (19 shorter events, 0.2 us)
Async XLA Ops:
  6.5 253.7 %copy-start = (bf16[4,4,512,128]{3,2,1,0:T(8,128)(2,1)S(1)}, bf16[4,4,512,128]{3,2,1,0:T(8,128)(2,1)}, u32[]{:S(2)}) copy-start(bf16[4,4,512,128]{3,2,1,0:T(8,128)(2,1)} %param.14) | copy-start | bytes 6291460
  6.5 3.0 %copy-start.1 = (s32[128]{0:T(128)S(1)}, s32[128]{0:T(128)}, u32[]{:S(2)}) copy-start(s32[128]{0:T(128)} %param.19) | copy-start | bytes 1540
  6.5 54.3 %all-gather.4.cloned.1.call-start = ((), (), s32[]{:S(2)}) async-start(), calls=%async_computation.1 | async-start | bytes 1114112 | tf_op jit(solution)/shard_map/all_gather | solution.py:101
  7.3 97.3 %all-gather.8.cloned.1.call-start = ((), (), s32[]{:S(2)}) async-start(), calls=%async_computation.3 | async-start | bytes 4456448 | tf_op jit(solution)/shard_map/all_gather | solution.py:77
  8.0 152.9 %all-gather.6.cloned.1.call-start = ((), (), s32[]{:S(2)}) async-start(), calls=%async_computation.2 | async-start | bytes 8912896 | tf_op jit(solution)/shard_map/all_gather | solution.py:76
  9.6 2.0 copy-start.4
  9.6 3.5 %copy-start.3 = (s32[64]{0:T(128)S(1)}, s32[64]{0:T(128)}, u32[]{:S(2)}) copy-start(s32[64]{0:T(128)} %param.17) | copy-start | bytes 772
  109.0 64.2 %copy-start.2 = (bf16[64,512]{1,0:T(8,128)(2,1)S(1)}, bf16[64,512]{1,0:T(8,128)(2,1)}, u32[]{:S(2)}) copy-start(bf16[64,512]{1,0:T(8,128)(2,1)} %param.10) | copy-start | bytes 196612
  245.1 15.2 %all-to-all-start = ((bf16[16,4,256]{2,1,0:T(4,128)(2,1)}), bf16[16,4,256]{2,1,0:T(4,128)(2,1)S(1)}, u32[]{:S(2)}, u32[]{:S(2)}) async-start(bf16[16,4,256]{2,1,0:T(4,128)(2,1)} %convert_element_type.34), calls=%async_computation | async-start | bytes 65536 | tf_op jit(solution)/shard_map/all_to_all | solution.py:113
Sparse Core Ops, SparseCore 0:
  9.8 50.9 all-gather.3
  62.6 41.8 all-gather.7
  106.3 54.4 all-gather.5
where the time goes:
time: 271 us; the launch traced here: 270 us
  waiting for transfers between devices  148 us (55%)
  blocking collectives  69.3 us (26%)
  matrix products  24.4 us (9%)
  between operations  13.2 us (5%)
  starting transfers between devices  8.97 us (3%)
  local copies, waits for them, and re-layouts  3.48 us (1%)
  other arithmetic  2.99 us (1%)
    psum x1, blocking collectives, sum_shrink(): return lax.psum(partial_pick, 'tensor').astype(jnp.bfloat16)  69.3 us
    all_gather x1, waiting for transfers between devices, on_device(): lax.all_gather(adapter_down, 'serve', axis=0, tiled=True)  51.8 us
    all_gather x1, waiting for transfers between devices, on_device(): lax.all_gather(hidden, 'tensor', axis=1, tiled=True)  47.5 us
    all_gather x1, waiting for transfers between devices, on_device(): lax.all_gather(adapter_up, 'serve', axis=0, tiled=True)  40.4 us
    dot_general x1, matrix products, on_device(): jnp.einsum('sa,adk->sdk', chosen, pieces[0], preferred_element_type=jnp.f...  12.4 us
    all_to_all x1, starting transfers between devices, on_device(): lax.all_to_all(query_rows, 'tensor', split_axis=0, concat_axis=1, tiled=T...  8.89 us
    all_to_all x1, waiting for transfers between devices, on_device(): lax.all_to_all(query_rows, 'tensor', split_axis=0, concat_axis=1, tiled=T...  6.23 us
  transfers between devices with their start and end apart: 4, of which 4 were waited for; matrix products, arithmetic and copies ran while one was open for 5% of the time, Pallas kernels for 0%

commit v1 on v0

v1 whole, which is shorter than its diff:
```python
import functools
import math

import jax
import jax.numpy as jnp
from jax import lax
from jax.experimental import pallas as pl
from jax.experimental.pallas import tpu as pltpu
from jax.sharding import PartitionSpec as P

ADAPTER_SCALE = 0.5
ROPE_BASE = 500000.0
NEG_LARGE = -1e30
BF = jnp.bfloat16
F32 = jnp.float32
CORES = 2
SLOTS_PER_CHIP = 4


def vmem_specs(count):
    return [pl.BlockSpec(memory_space=pltpu.VMEM) for _ in range(count)]


def lane(shape):
    return lax.broadcasted_iota(jnp.int32, shape, len(shape) - 1)


def pack_down_kernel(down_ref, out_ref):
    for pair in range(down_ref.shape[0] // 2):
        out_ref[:, pair * 128 : pair * 128 + 128] = jnp.concatenate(
            [down_ref[2 * pair], down_ref[2 * pair + 1]], axis=1
        )


def pack_down(adapter_down):
    count, depth, rank = adapter_down.shape
    return pl.pallas_call(
        pack_down_kernel,
        out_shape=jax.ShapeDtypeStruct((depth, count * rank), BF),
        in_specs=vmem_specs(1),
        out_specs=vmem_specs(1)[0],
    )(adapter_down)


def home_kernel(first_ref, source_ref, message_ref, own_down, other_down, own_up, other_up, out_ref):
    depth = own_down.shape[0]
    rows = message_ref.shape[0]
    hidden = message_ref[:, :depth]
    wanted = message_ref[:, depth:].astype(F32)
    half = (lane((rows, 128)) >= 64).astype(F32)
    total = jnp.zeros((rows, 128), F32)
    for side, down in enumerate((own_down, other_down)):
        product = jnp.dot(hidden, down[...], preferred_element_type=F32)
        first = first_ref[side].astype(F32)
        for pair in range(product.shape[1] // 128):
            here = wanted == first + (2.0 * pair) + half
            total += jnp.where(here, product[:, pair * 128 : pair * 128 + 128], 0.0)
    total = total + pltpu.roll(total, 64, 1)
    high = total.astype(BF).astype(F32)
    low = (total - high).astype(BF).astype(F32)
    both = jnp.where(half > 0.5, low, high).astype(BF)
    out_ref[:32, :128] = both[:32]
    out_ref[:32, 128:] = both[32:]
    for slot in range(SLOTS_PER_CHIP):
        source = source_ref[slot]
        at = 32 + 64 * slot

        @pl.when(source < 8)
        def _():
            out_ref[at : at + 64, :] = own_up[jnp.minimum(source, 7)]

        @pl.when(source >= 8)
        def _():
            out_ref[at : at + 64, :] = other_up[jnp.maximum(source - 8, 0)]


def home_step(first, source, message, own_down, other_down, own_up, other_up):
    return pl.pallas_call(
        home_kernel,
        out_shape=jax.ShapeDtypeStruct((32 + 64 * SLOTS_PER_CHIP, 256), BF),
        in_specs=[pl.BlockSpec(memory_space=pltpu.SMEM)] * 2 + vmem_specs(5),
        out_specs=vmem_specs(1)[0],
    )(first, source, message, own_down, other_down, own_up, other_up)


def collect_kernel(*refs):
    out_ref = refs[-1]
    total = refs[0][:32, :].astype(F32)
    for ref in refs[1:-1]:
        total += ref[:32, :].astype(F32)
    total = total.astype(BF)
    for place in range(out_ref.shape[0]):
        out_ref[place] = total


def collect(replies, copies):
    return pl.pallas_call(
        collect_kernel,
        out_shape=jax.ShapeDtypeStruct((copies, 32, 256), BF),
        in_specs=vmem_specs(len(replies)),
        out_specs=vmem_specs(1)[0],
    )(*replies)


def base_kernel(hidden_ref, weight_ref, out_ref):
    @pl.when(pl.program_id(0) == 0)
    def _():
        out_ref[...] = jnp.zeros_like(out_ref)

    out_ref[...] += jnp.dot(hidden_ref[0], weight_ref[...], preferred_element_type=F32)


def base_product(hidden_all, weight):
    parts, rows, depth = hidden_all.shape
    columns = weight.shape[1]
    return pl.pallas_call(
        base_kernel,
        grid=(parts,),
        out_shape=jax.ShapeDtypeStruct((rows, columns), F32),
        in_specs=[
            pl.BlockSpec((1, rows, depth), lambda i: (i, 0, 0)),
            pl.BlockSpec((depth, columns), lambda i: (i, 0)),
        ],
        out_specs=pl.BlockSpec((rows, columns), lambda i: (0, 0)),
    )(hidden_all, weight)


def finish_kernel(partial_ref, table_ref, wanted_ref, base_ref, cos_ref, sin_ref, *refs):
    out_ref = refs[-1]
    replies = refs[:-1]
    total = partial_ref[0].astype(F32)
    for place in range(1, partial_ref.shape[0]):
        total += partial_ref[place].astype(F32)
    total = jnp.concatenate([total[:, :128], total[:, 128:]], axis=0)
    shrunk = (total + pltpu.roll(total, 64, 1)).astype(BF).astype(F32)
    shrunk = jnp.concatenate([shrunk, shrunk], axis=1)
    wanted = wanted_ref[...]
    query = jnp.zeros(base_ref.shape, F32)
    for place, reply in enumerate(replies):
        here = wanted == table_ref[place : place + 1, :]
        wide = jnp.where(here, shrunk, 0.0).astype(BF)
        query += jnp.dot(wide, reply[32:, :], preferred_element_type=F32)
    query = base_ref[...] + ADAPTER_SCALE * query
    for head in range(query.shape[1] // 128):
        piece = query[:, head * 128 : head * 128 + 128]
        turned = piece * cos_ref[...] + pltpu.roll(piece, 64, 1) * sin_ref[...]
        out_ref[:, head * 128 : head * 128 + 128] = turned.astype(BF)


def finish(partials, table, wanted, base, cosine, sine, replies):
    return pl.pallas_call(
        finish_kernel,
        out_shape=jax.ShapeDtypeStruct(base.shape, BF),
        in_specs=vmem_specs(6 + len(replies)),
        out_specs=vmem_specs(1)[0],
    )(partials, table, wanted, base, cosine, sine, *replies)


def rotation(positions, head_dim):
    half_width = head_dim // 2
    exponent = jnp.arange(half_width, dtype=F32) * (2.0 / head_dim)
    inverse = jnp.exp(-math.log(ROPE_BASE) * exponent)
    angles = positions.astype(F32)[:, None] * inverse[None, :]
    cosine, sine = jnp.cos(angles), jnp.sin(angles)
    return (
        jnp.concatenate([cosine, cosine], axis=1),
        jnp.concatenate([-sine, sine], axis=1),
    )


def attend_rows(row_query, rotated_key_cache, cached_value_rows, lengths):
    local_rows, kv_heads, cache_count, head_dim = rotated_key_cache.shape
    grouped = row_query.reshape(local_rows, kv_heads, -1, head_dim)
    scores = jnp.einsum(
        "rkgd,rktd->rkgt", grouped, rotated_key_cache, preferred_element_type=F32
    ) * head_dim ** (-0.5)
    valid_mask = (jnp.arange(cache_count)[None, :] < lengths[:, None])[:, None, None, :]
    row_max = jnp.max(jnp.where(valid_mask, scores, NEG_LARGE), axis=3, keepdims=True)
    weights = jnp.where(valid_mask, jnp.exp(scores - row_max), 0.0).astype(BF)
    totals = jnp.sum(weights.astype(F32), axis=3)
    numerator = jnp.einsum(
        "rkgt,rktd->rkgd", weights, cached_value_rows, preferred_element_type=F32
    )
    return (numerator / totals[..., None]).reshape(local_rows, -1).astype(BF)


def slot_table(group_adapters, adapter_pool_row, chips):
    live = group_adapters >= 0
    ids = jnp.arange(adapter_pool_row.shape[0], dtype=jnp.int32)
    rows = jnp.sum(
        jnp.where(group_adapters[:, :, None] == ids, adapter_pool_row[None, None, :], 0), axis=2
    )
    chip = jnp.where(live, rows // 16, -1)
    count = group_adapters.shape[1]
    earlier = jnp.arange(count)[None, :] < jnp.arange(count)[:, None]
    rank = jnp.sum(
        jnp.where((chip[:, :, None] == chip[:, None, :]) & earlier[None], 1, 0), axis=2
    )
    here = (chip[:, None, None, :] == jnp.arange(chips)[None, :, None, None]) & (
        rank[:, None, None, :] == jnp.arange(SLOTS_PER_CHIP)[None, None, :, None]
    )
    return jnp.sum(jnp.where(here, rows[:, None, None, :] + 1, 0), axis=3) - 1


def on_device(
    hidden,
    query_weight,
    adapter_down,
    adapter_up,
    rotated_key_cache,
    cached_value_rows,
    cached_length,
    request_adapter,
    group_adapters,
    adapter_pool_row,
):
    group = lax.axis_index("serve")
    tensor_index = lax.axis_index("tensor")
    serve_size = lax.axis_size("serve")
    tensor_size = lax.axis_size("tensor")
    chips = serve_size // CORES
    chip, core = group // CORES, group % CORES
    rows = hidden.shape[0]
    head_dim = rotated_key_cache.shape[3]
    local_rows = rotated_key_cache.shape[0]

    def along(array, steps):
        return lax.ppermute(
            array,
            "serve",
            [(i, (i // 2 + steps) % chips * 2 + i % 2) for i in range(serve_size)],
        )

    def other_core(array):
        return lax.ppermute(array, "serve", [(i, i ^ 1) for i in range(serve_size)])

    ids = jnp.arange(adapter_pool_row.shape[0], dtype=jnp.int32)
    wanted = jnp.sum(
        jnp.where(request_adapter[:, None] == ids, adapter_pool_row[None, :], 0), axis=1
    )
    message = jnp.concatenate(
        [hidden, jnp.broadcast_to(wanted.astype(BF)[:, None], (rows, 128))], axis=1
    )
    own_down = pack_down(adapter_down)
    other_down = other_core(own_down)
    other_up = other_core(adapter_up)
    hidden_all = lax.all_to_all(
        jnp.broadcast_to(hidden[None], (tensor_size,) + hidden.shape), "tensor", 0, 0
    )
    arrived = [message] + [along(message, d) for d in range(1, chips)]

    table = slot_table(group_adapters, adapter_pool_row, chips)
    distance = jnp.arange(chips)
    asking = (chip - distance) % chips * CORES + core
    answering = (chip + distance) % chips
    by_chip = jnp.sum(
        jnp.where((distance == chip)[None, :, None], table, 0), axis=1
    )
    source = jnp.sum(
        jnp.where(
            (asking[:, None] == jnp.arange(serve_size)[None, :])[:, :, None], by_chip[None], 0
        ),
        axis=1,
    )
    source = jnp.maximum(source, 0)
    source = (source % 8) + 8 * ((source // 8 % 2) ^ core)
    my_table = lax.dynamic_index_in_dim(table, group, 0, keepdims=False)
    my_table = jnp.sum(
        jnp.where((answering[:, None] == distance[None, :])[:, :, None], my_table[None], 0), axis=1
    )
    my_table = jnp.repeat(my_table.astype(F32), 64, axis=1)
    first = jnp.stack([group * 8, (group ^ 1) * 8]).astype(jnp.int32)

    replies = []
    for d in range(chips):
        reply = home_step(
            first, source[d], arrived[d], own_down, other_down, adapter_up, other_up
        )
        replies.append(along(reply, -d) if d else reply)
    partials = lax.all_to_all(collect(replies, tensor_size), "tensor", 0, 0)
    base = base_product(hidden_all, query_weight)
    cosine, sine = rotation(cached_length, head_dim)
    wanted_wide = jnp.broadcast_to(wanted.astype(F32)[:, None], (rows, 256))
    query_rows = finish(partials, my_table, wanted_wide, base, cosine, sine, replies)
    row_query = lax.all_to_all(query_rows, "tensor", split_axis=0, concat_axis=1, tiled=True)
    lengths = lax.dynamic_slice_in_dim(cached_length, tensor_index * local_rows, local_rows, 0)
    return attend_rows(row_query, rotated_key_cache, cached_value_rows, lengths)


def solution(mesh):
    placed = (
        P("serve", "tensor"),
        P(None, "tensor"),
        P("serve", "tensor", None),
        P("serve", None, "tensor"),
        P(("serve", "tensor"), None, None, None),
        P(("serve", "tensor"), None, None, None),
        P("serve"),
        P("serve"),
        P(),
        P(),
    )
    return jax.shard_map(
        on_device,
        mesh=mesh,
        in_specs=placed,
        out_specs=P(("serve", "tensor"), None),
        check_vma=False,
    )
```

time: 271 us -> 130 us (0.48)
  waiting for transfers between devices: 148 us -> 19.4 us
  blocking collectives: 69.3 us -> 0 us
  starting transfers between devices: 8.97 us -> 53.3 us
  Pallas kernels: 0 us -> 36.8 us
  matrix products: 24.4 us -> 1.01 us
  between operations: 13.2 us -> 0.29 us
  local copies, waits for them, and re-layouts: 3.48 us -> 11 us
  other arithmetic: 2.99 us -> 6.66 us
    all_gather x3 -> x0, waiting for transfers between devices: 140 us -> none  [the longest x1 51.8 us: on_device(): lax.all_gather(adapter_down, 'serve', axis=0, tiled=True)]
    psum x1 -> x0, blocking collectives: 69.3 us -> none  [sum_shrink(): return lax.psum(partial_pick, 'tensor').astype(jnp.bfloat16)]
    pallas_call x0 -> x12, Pallas kernels: none -> 36.8 us  [the longest x8 19.7 us: home_step(): pl.pallas_call(home_kernel, out_shape=jax.ShapeDtypeStruct((32 + 64 * SLO...]
    ppermute x0 -> x16, starting transfers between devices: none -> 31.4 us  [the longest x14 30.9 us: along(): lax.ppermute(array, 'serve', [(i, (i // 2 + steps) % chips * 2 + i % 2) f...]
    dot_general x5 -> x0, matrix products: 21.8 us -> none  [the longest x1 12.4 us: on_device(): jnp.einsum('sa,adk->sdk', chosen, pieces[0], preferred_element_type=jnp.f...]
    all_to_all x0 -> x2, starting transfers between devices: none -> 14.7 us  [the longest x1 7.48 us: on_device(): lax.all_to_all(jnp.broadcast_to(hidden[None], (tensor_size,) + hidden.sha...]
    ppermute x0 -> x16, waiting for transfers between devices: none -> 13.3 us  [the longest x14 13.2 us: along(): lax.ppermute(array, 'serve', [(i, (i // 2 + steps) % chips * 2 + i % 2) f...]
    unnamed x11 -> x48, local copies, waits for them, and re-layouts: 0.68 us -> 5.86 us
  transfers between devices with their start and end apart: 4 -> 19, of which waited for: 4 -> 4; matrix products, arithmetic and copies ran while one was open for 5% -> 8% of each run, Pallas kernels for 0% -> 27%
where the time goes in v1:
time: 130 us; the launch traced here: 129 us
  starting transfers between devices  53.3 us (41%)
  Pallas kernels  36.8 us (28%)
  waiting for transfers between devices  19.4 us (15%)
  local copies, waits for them, and re-layouts  11 us (8%)
  other arithmetic  6.66 us (5%)
    ppermute x14, starting transfers between devices, along(): lax.ppermute(array, 'serve', [(i, (i // 2 + steps) % chips * 2 + i % 2) f...  30.9 us
    pallas_call x8, Pallas kernels, home_step(): pl.pallas_call(home_kernel, out_shape=jax.ShapeDtypeStruct((32 + 64 * SLO...  19.7 us
    ppermute x14, waiting for transfers between devices, along(): lax.ppermute(array, 'serve', [(i, (i // 2 + steps) % chips * 2 + i % 2) f...  13.2 us
    pallas_call x1, Pallas kernels, base_product(): pl.pallas_call(base_kernel, grid=(parts,), out_shape=jax.ShapeDtypeStruct...  10.3 us
    all_to_all x1, starting transfers between devices, on_device(): lax.all_to_all(jnp.broadcast_to(hidden[None], (tensor_size,) + hidden.sha...  7.48 us
    all_to_all x1, starting transfers between devices, on_device(): lax.all_to_all(query_rows, 'tensor', split_axis=0, concat_axis=1, tiled=T...  7.23 us
    all_to_all x1, starting transfers between devices, on_device(): partials = lax.all_to_all(collect(replies, tensor_size), 'tensor', 0, 0)  7.23 us
    all_to_all x1, waiting for transfers between devices, on_device(): lax.all_to_all(query_rows, 'tensor', split_axis=0, concat_axis=1, tiled=T...  6.17 us
  transfers between devices with their start and end apart: 19, of which 4 were waited for; matrix products, arithmetic and copies ran while one was open for 8% of the time, Pallas kernels for 27%

profile of v1, /device:TPU:2, one launch (start us, length us, event | category | flops | bytes accessed | tf_op | source)
XLA Modules:
  0.0 128.6 jit_solution(13238108490848820049)
XLA Ops:
  2.0 2.0 %collective-permute-start.2 = (bf16[64,640]{1,0:T(8,128)(2,1)S(1)}, bf16[64,640]{1,0:T(8,128)(2,1)S(1)}, u32[]{:S(2)}, u32[]{:S(2)}) collective-permute-start(bf16[64,640]{1,0:T(8,128)(2,1)S(1)} %pad_maximum_fusion.message_ref), channel_id=1, source_target_pairs={{0,32},{16,48},{32,64},{48,80},{64,96},{80,112},{96,128},{112,144}... | collective-permute-start | bytes 245768 | tf_op jit(solution)/shard_map/ppermute | solution.py:228
  4.0 3.3 %collective-permute-start.4 = (bf16[64,640]{1,0:T(8,128)(2,1)S(1)}, bf16[64,640]{1,0:T(8,128)(2,1)S(1)}, u32[]{:S(2)}, u32[]{:S(2)}) collective-permute-start(bf16[64,640]{1,0:T(8,128)(2,1)S(1)} %pad_maximum_fusion.message_ref), channel_id=1, source_target_pairs={{0,64},{16,80},{32,96},{48,112},{64,128},{80,144},{96,160},{112,17... | collective-permute-start | bytes 245768 | tf_op jit(solution)/shard_map/ppermute | solution.py:228
  7.2 4.0 %collective-permute-start.6 = (bf16[64,640]{1,0:T(8,128)(2,1)S(1)}, bf16[64,640]{1,0:T(8,128)(2,1)S(1)}, u32[]{:S(2)}, u32[]{:S(2)}) collective-permute-start(bf16[64,640]{1,0:T(8,128)(2,1)S(1)} %pad_maximum_fusion.message_ref), channel_id=1, source_target_pairs={{0,96},{16,112},{32,128},{48,144},{64,160},{80,176},{96,192},{112,... | collective-permute-start | bytes 245768 | tf_op jit(solution)/shard_map/ppermute | solution.py:228
  11.3 2.4 %copy.21.down_ref = bf16[8,512,64]{2,1,0:T(8,128)(2,1)} copy(bf16[8,512,64]{1,2,0:T(8,128)(2,1)} %param.12) | data formatting | bytes 1048576 | tf_op args[2]
  13.6 2.2 %shard_map.100.own_down = bf16[512,512]{1,0:T(8,128)(2,1)} custom-call(bf16[8,512,64]{2,1,0:T(8,128)(2,1)} %copy.21.down_ref), custom_call_target="tpu_custom_call" | custom-call | tf_op jit(solution)/shard_map/pallas_call | solution.py:37
  16.4 1.1 broadcast_in_dim.192
  17.5 7.5 %all-to-all-start.1 = ((bf16[16,64,512]{2,1,0:T(8,128)(2,1)}), bf16[16,64,512]{2,1,0:T(8,128)(2,1)}, u32[]{:S(2)}, u32[]{:S(2)}) async-start(bf16[16,64,512]{2,1,0:T(8,128)(2,1)} %broadcast_in_dim.192), calls=%async_computation.1 | async-start | bytes 2097152 | tf_op jit(solution)/shard_map/all_to_all | solution.py:247
  26.0 1.2 select_reduce_fusion.1
  30.0 4.9 %collective-permute-start.10 = (bf16[64,640]{1,0:T(8,128)(2,1)S(1)}, bf16[64,640]{1,0:T(8,128)(2,1)}, u32[]{:S(2)}, u32[]{:S(2)}) collective-permute-start(bf16[64,640]{1,0:T(8,128)(2,1)S(1)} %pad_maximum_fusion.message_ref), channel_id=1, source_target_pairs={{0,160},{16,176},{32,192},{48,208},{64,224},{80,240},{96,0},{112,1... | collective-permute-start | bytes 245768 | tf_op jit(solution)/shard_map/ppermute | solution.py:228
  35.7 2.5 %shard_map.102 = bf16[288,256]{1,0:T(8,128)(2,1)} custom-call(s32[2]{0:T(128)} %pad_add_fusion.first_ref, s32[4]{0:T(128)} %get-tuple-element.11.source_ref, bf16[64,640]{1,0:T(8,128)(2,1)} %copy-done.17, bf16[512,512]{1,0:T(8,128)(2,1)} %shard_map.100.own_down, bf16[512,512]{1,0:T(8,128)(2,1)} %copy-done.1, bf16[8,64,256]{2,1,0:T(8,128)(2,1)} %own_up.15, ...), custom_call_target="tpu_custom_call" | custom-call | tf_op jit(solution)/shard_map/pallas_call | solution.py:78
  39.8 2.5 %shard_map.103 = bf16[288,256]{1,0:T(8,128)(2,1)} custom-call(s32[2]{0:T(128)} %pad_add_fusion.first_ref, s32[4]{0:T(128)} %get-tuple-element.10.source_ref, bf16[64,640]{1,0:T(8,128)(2,1)} %copy-done.16, bf16[512,512]{1,0:T(8,128)(2,1)} %shard_map.100.own_down, bf16[512,512]{1,0:T(8,128)(2,1)} %copy-done.1, bf16[8,64,256]{2,1,0:T(8,128)(2,1)} %own_up.15, ...), custom_call_target="tpu_custom_call" | custom-call | tf_op jit(solution)/shard_map/pallas_call | solution.py:78
  42.3 2.7 %collective-permute-start.5 = (bf16[288,256]{1,0:T(8,128)(2,1)}, bf16[288,256]{1,0:T(8,128)(2,1)S(1)}, u32[]{:S(2)}, u32[]{:S(2)}) collective-permute-start(bf16[288,256]{1,0:T(8,128)(2,1)} %shard_map.103), channel_id=1, source_target_pairs={{0,192},{16,208},{32,224},{48,240},{64,0},{80,16},{96,32},{112,48}... | collective-permute-start | bytes 442376 | tf_op jit(solution)/shard_map/ppermute | solution.py:228
  46.1 2.5 %shard_map.104 = bf16[288,256]{1,0:T(8,128)(2,1)} custom-call(s32[2]{0:T(128)} %pad_add_fusion.first_ref, s32[4]{0:T(128)} %get-tuple-element.9.source_ref, bf16[64,640]{1,0:T(8,128)(2,1)} %copy-done.15, bf16[512,512]{1,0:T(8,128)(2,1)} %shard_map.100.own_down, bf16[512,512]{1,0:T(8,128)(2,1)} %copy-done.1, bf16[8,64,256]{2,1,0:T(8,128)(2,1)} %own_up.15, ...), custom_call_target="tpu_custom_call" | custom-call | tf_op jit(solution)/shard_map/pallas_call | solution.py:78
  48.6 2.5 %shard_map.105 = bf16[288,256]{1,0:T(8,128)(2,1)} custom-call(s32[2]{0:T(128)} %pad_add_fusion.first_ref, s32[4]{0:T(128)} %get-tuple-element.8.source_ref, bf16[64,640]{1,0:T(8,128)(2,1)} %collective-permute-done.8.message_ref, bf16[512,512]{1,0:T(8,128)(2,1)} %shard_map.100.own_down, bf16[512,512]{1,0:T(8,128)(2,1)} %copy-done.1, ...), custom_call_target="tpu_custom_call" | custom-call | tf_op jit(solution)/shard_map/pallas_call | solution.py:78
  51.0 3.4 %collective-permute-start.7 = (bf16[288,256]{1,0:T(8,128)(2,1)}, bf16[288,256]{1,0:T(8,128)(2,1)S(1)}, u32[]{:S(2)}, u32[]{:S(2)}) collective-permute-start(bf16[288,256]{1,0:T(8,128)(2,1)} %shard_map.104), channel_id=1, source_target_pairs={{0,160},{16,176},{32,192},{48,208},{64,224},{80,240},{96,0},{112,1... | collective-permute-start | bytes 442376 | tf_op jit(solution)/shard_map/ppermute | solution.py:228
  54.4 2.5 %shard_map.106 = bf16[288,256]{1,0:T(8,128)(2,1)} custom-call(s32[2]{0:T(128)} %pad_add_fusion.first_ref, s32[4]{0:T(128)} %get-tuple-element.7.source_ref, bf16[64,640]{1,0:T(8,128)(2,1)} %collective-permute-done.10.message_ref, bf16[512,512]{1,0:T(8,128)(2,1)} %shard_map.100.own_down, bf16[512,512]{1,0:T(8,128)(2,1)} %copy-done.1, ...), custom_call_target="tpu_custom_call" | custom-call | tf_op jit(solution)/shard_map/pallas_call | solution.py:78
  56.9 2.3 %collective-permute-start.9 = (bf16[288,256]{1,0:T(8,128)(2,1)}, bf16[288,256]{1,0:T(8,128)(2,1)S(1)}, u32[]{:S(2)}, u32[]{:S(2)}) collective-permute-start(bf16[288,256]{1,0:T(8,128)(2,1)} %shard_map.105), channel_id=1, source_target_pairs={{0,128},{16,144},{32,160},{48,176},{64,192},{80,208},{96,224},{112... | collective-permute-start | bytes 442376 | tf_op jit(solution)/shard_map/ppermute | solution.py:228
  59.2 2.5 %shard_map.107 = bf16[288,256]{1,0:T(8,128)(2,1)} custom-call(s32[2]{0:T(128)} %pad_add_fusion.first_ref, s32[4]{0:T(128)} %get-tuple-element.6.source_ref, bf16[64,640]{1,0:T(8,128)(2,1)} %copy-done.19, bf16[512,512]{1,0:T(8,128)(2,1)} %shard_map.100.own_down, bf16[512,512]{1,0:T(8,128)(2,1)} %copy-done.1, bf16[8,64,256]{2,1,0:T(8,128)(2,1)} %own_up.15, ...), custom_call_target="tpu_custom_call" | custom-call | tf_op jit(solution)/shard_map/pallas_call | solution.py:78
  61.7 3.7 %collective-permute-start.11 = (bf16[288,256]{1,0:T(8,128)(2,1)}, bf16[288,256]{1,0:T(8,128)(2,1)S(1)}, u32[]{:S(2)}, u32[]{:S(2)}) collective-permute-start(bf16[288,256]{1,0:T(8,128)(2,1)} %shard_map.106), channel_id=1, source_target_pairs={{0,96},{16,112},{32,128},{48,144},{64,160},{80,176},{96,192},{112,... | collective-permute-start | bytes 442376 | tf_op jit(solution)/shard_map/ppermute | solution.py:228
  65.4 2.5 %shard_map.108 = bf16[288,256]{1,0:T(8,128)(2,1)} custom-call(s32[2]{0:T(128)} %pad_add_fusion.first_ref, s32[4]{0:T(128)} %get-tuple-element.5.source_ref, bf16[64,640]{1,0:T(8,128)(2,1)} %copy-done.18, bf16[512,512]{1,0:T(8,128)(2,1)} %shard_map.100.own_down, bf16[512,512]{1,0:T(8,128)(2,1)} %copy-done.1, bf16[8,64,256]{2,1,0:T(8,128)(2,1)} %own_up.15, ...), custom_call_target="tpu_custom_call" | custom-call | tf_op jit(solution)/shard_map/pallas_call | solution.py:78
  67.8 1.8 %collective-permute-start.13 = (bf16[288,256]{1,0:T(8,128)(2,1)}, bf16[288,256]{1,0:T(8,128)(2,1)S(1)}, u32[]{:S(2)}, u32[]{:S(2)}) collective-permute-start(bf16[288,256]{1,0:T(8,128)(2,1)} %shard_map.107), channel_id=1, source_target_pairs={{0,64},{16,80},{32,96},{48,112},{64,128},{80,144},{96,160},{112,17... | collective-permute-start | bytes 442376 | tf_op jit(solution)/shard_map/ppermute | solution.py:228
  70.9 2.5 %shard_map.101.refs_0_ = bf16[288,256]{1,0:T(8,128)(2,1)} custom-call(s32[2]{0:T(128)} %pad_add_fusion.first_ref, s32[4]{0:T(128)} %get-tuple-element.12.source_ref, bf16[64,640]{1,0:T(8,128)(2,1)} %copy-done.13, bf16[512,512]{1,0:T(8,128)(2,1)} %shard_map.100.own_down, bf16[512,512]{1,0:T(8,128)(2,1)} %copy-done.1, bf16[8,64,256]{2,1,0:T(8,128)(2,1)} %own_up.15, ...), custom_call_target="tpu_custom_call" | custom-call | tf_op jit(solution)/shard_map/pallas_call | solution.py:78
  73.4 6.1 %collective-permute-done.11.refs_5_ = bf16[288,256]{1,0:T(8,128)(2,1)S(1)} collective-permute-done((bf16[288,256]{1,0:T(8,128)(2,1)}, bf16[288,256]{1,0:T(8,128)(2,1)S(1)}, u32[]{:S(2)}, u32[]{:S(2)}) %collective-permute-start.11) | collective-permute-done | bytes 147488 | tf_op jit(solution)/shard_map/ppermute | solution.py:228
  79.5 4.9 %collective-permute-done.13.refs_6_ = bf16[288,256]{1,0:T(8,128)(2,1)S(1)} collective-permute-done((bf16[288,256]{1,0:T(8,128)(2,1)}, bf16[288,256]{1,0:T(8,128)(2,1)S(1)}, u32[]{:S(2)}, u32[]{:S(2)}) %collective-permute-start.13) | collective-permute-done | bytes 147488 | tf_op jit(solution)/shard_map/ppermute | solution.py:228
  84.5 2.2 %collective-permute-done.15.refs_7_ = bf16[288,256]{1,0:T(8,128)(2,1)S(1)} collective-permute-done((bf16[288,256]{1,0:T(8,128)(2,1)}, bf16[288,256]{1,0:T(8,128)(2,1)S(1)}, u32[]{:S(2)}, u32[]{:S(2)}) %collective-permute-start.15) | collective-permute-done | bytes 147488 | tf_op jit(solution)/shard_map/ppermute | solution.py:228
  87.3 2.1 %shard_map.109 = bf16[16,32,256]{2,1,0:T(8,128)(2,1)} custom-call(bf16[288,256]{1,0:T(8,128)(2,1)} %shard_map.101.refs_0_, bf16[288,256]{1,0:T(8,128)(2,1)} %copy-done.6, bf16[288,256]{1,0:T(8,128)(2,1)} %copy-done.7, bf16[288,256]{1,0:T(8,128)(2,1)} %copy-done.8, bf16[288,256]{1,0:T(8,128)(2,1)} %copy-done.9, bf16[288,256]{1,0:T(8,128)(2,1)} %copy-done.10, ...), custom_call_target="tpu_custom_call" | custom-call | tf_op jit(solution)/shard_map/pallas_call | solution.py:97
  89.4 7.2 %all-to-all-start = ((bf16[16,32,256]{2,1,0:T(8,128)(2,1)}), bf16[16,32,256]{2,1,0:T(8,128)(2,1)S(1)}, u32[]{:S(2)}, u32[]{:S(2)}) async-start(bf16[16,32,256]{2,1,0:T(8,128)(2,1)} %shard_map.109), calls=%async_computation | async-start | bytes 524288 | tf_op jit(solution)/shard_map/all_to_all | solution.py:280
  97.6 10.3 %shard_map.110.base_ref = f32[64,256]{1,0:T(8,128)} custom-call(bf16[16,64,512]{2,1,0:T(8,128)(2,1)} %all-to-all-done.1.hidden_ref, bf16[8192,256]{1,0:T(8,128)(2,1)} %weight_ref.1), custom_call_target="tpu_custom_call" | custom-call | tf_op jit(solution)/shard_map/pallas_call | solution.py:116
  108.6 2.5 %shard_map.111 = bf16[64,256]{1,0:T(8,128)(2,1)} custom-call(bf16[16,32,256]{2,1,0:T(8,128)(2,1)} %copy-done.5, f32[8,256]{1,0:T(8,128)} %reshape.159.table_ref, f32[64,256]{1,0:T(8,128)} %broadcast_in_dim.191.wanted_ref, f32[64,256]{1,0:T(8,128)} %shard_map.110.base_ref, f32[64,128]{1,0:T(8,128)} %get-tuple-element.26.cos_ref, ...), custom_call_target="tpu_custom_call" | custom-call | tf_op jit(solution)/shard_map/pallas_call | solution.py:151
  111.1 1.4 %all_to_all.20 = bf16[16,4,256]{2,1,0:T(4,128)(2,1)} reshape(bf16[64,256]{1,0:T(8,128)(2,1)} %shard_map.111) | data formatting | bytes 65536 | tf_op jit(solution)/shard_map/all_to_all | solution.py:285
  112.5 7.2 %all-to-all-start.2 = ((bf16[16,4,256]{2,1,0:T(4,128)(2,1)}), bf16[16,4,256]{2,1,0:T(4,128)(2,1)S(1)}, u32[]{:S(2)}, u32[]{:S(2)}) async-start(bf16[16,4,256]{2,1,0:T(4,128)(2,1)} %all_to_all.20), calls=%async_computation.2 | async-start | bytes 65536 | tf_op jit(solution)/shard_map/all_to_all | solution.py:285
  119.8 6.2 %all-to-all-done.2 = bf16[16,4,256]{2,1,0:T(4,128)(2,1)S(1)} async-done(((bf16[16,4,256]{2,1,0:T(4,128)(2,1)}), bf16[16,4,256]{2,1,0:T(4,128)(2,1)S(1)}, u32[]{:S(2)}, u32[]{:S(2)}) %all-to-all-start.2) | async-done | bytes 32800 | tf_op jit(solution)/shard_map/all_to_all | solution.py:285
  (107 shorter events, 16.0 us)
Async XLA Ops:
  0.0 126.0 %copy-start = (bf16[4,4,512,128]{3,2,1,0:T(8,128)(2,1)S(1)}, bf16[4,4,512,128]{3,2,1,0:T(8,128)(2,1)}, u32[]{:S(2)}) copy-start(bf16[4,4,512,128]{3,2,1,0:T(8,128)(2,1)} %param.14) | copy-start | bytes 6291460
  0.0 16.4 %copy-start.14 = (bf16[64,512]{1,0:T(8,128)(2,1)S(1)}, bf16[64,512]{1,0:T(8,128)(2,1)}, u32[]{:S(2)}) copy-start(bf16[64,512]{1,0:T(8,128)(2,1)} %param.10) | copy-start | bytes 196612
  0.0 15.9 %copy-start.2 = (bf16[8,64,256]{2,1,0:T(8,128)(2,1)S(1)}, bf16[8,64,256]{2,1,0:T(8,128)(2,1)}, u32[]{:S(2)}) copy-start(bf16[8,64,256]{2,1,0:T(8,128)(2,1)} %own_up.15) | copy-start | bytes 786436
  2.0 43.1 %copy-start.13 = (bf16[64,640]{1,0:T(8,128)(2,1)}, bf16[64,640]{1,0:T(8,128)(2,1)S(1)}, u32[]{:S(2)}) copy-start(bf16[64,640]{1,0:T(8,128)(2,1)S(1)} %pad_maximum_fusion.message_ref) | copy-start | bytes 245764
  2.0 27.4 %collective-permute-start.2 = (bf16[64,640]{1,0:T(8,128)(2,1)S(1)}, bf16[64,640]{1,0:T(8,128)(2,1)S(1)}, u32[]{:S(2)}, u32[]{:S(2)}) collective-permute-start(bf16[64,640]{1,0:T(8,128)(2,1)S(1)} %pad_maximum_fusion.message_ref), channel_id=1, source_target_pairs={{0,32},{16,48},{32,64},{48,80},{64,96},{80,112},{96,128},{112,144}... | collective-permute-start | bytes 245768 | tf_op jit(solution)/shard_map/ppermute | solution.py:228
  4.0 35.2 %collective-permute-start.4 = (bf16[64,640]{1,0:T(8,128)(2,1)S(1)}, bf16[64,640]{1,0:T(8,128)(2,1)S(1)}, u32[]{:S(2)}, u32[]{:S(2)}) collective-permute-start(bf16[64,640]{1,0:T(8,128)(2,1)S(1)} %pad_maximum_fusion.message_ref), channel_id=1, source_target_pairs={{0,64},{16,80},{32,96},{48,112},{64,128},{80,144},{96,160},{112,17... | collective-permute-start | bytes 245768 | tf_op jit(solution)/shard_map/ppermute | solution.py:228
  7.2 37.8 %collective-permute-start.6 = (bf16[64,640]{1,0:T(8,128)(2,1)S(1)}, bf16[64,640]{1,0:T(8,128)(2,1)S(1)}, u32[]{:S(2)}, u32[]{:S(2)}) collective-permute-start(bf16[64,640]{1,0:T(8,128)(2,1)S(1)} %pad_maximum_fusion.message_ref), channel_id=1, source_target_pairs={{0,96},{16,112},{32,128},{48,144},{64,160},{80,176},{96,192},{112,... | collective-permute-start | bytes 245768 | tf_op jit(solution)/shard_map/ppermute | solution.py:228
  13.6 11.4 %copy-start.20 = (s32[16,16]{1,0:T(8,128)S(1)}, s32[16,16]{1,0:T(8,128)}, u32[]{:S(2)}) copy-start(s32[16,16]{1,0:T(8,128)} %param.18) | copy-start | bytes 3076
  13.6 11.4 %copy-start.21 = (s32[128]{0:T(128)S(1)}, s32[128]{0:T(128)}, u32[]{:S(2)}) copy-start(s32[128]{0:T(128)} %param.19) | copy-start | bytes 1540
  15.9 19.0 %collective-permute-start = (bf16[512,512]{1,0:T(8,128)(2,1)}, bf16[512,512]{1,0:T(8,128)(2,1)S(1)}, u32[]{:S(2)}, u32[]{:S(2)}) collective-permute-start(bf16[512,512]{1,0:T(8,128)(2,1)} %shard_map.100.own_down), channel_id=1, source_target_pairs={{0,16},{16,0},{32,48},{48,32},{64,80},{80,64},{96,112},{112,96},{1... | collective-permute-start | bytes 1572872 | tf_op jit(solution)/shard_map/ppermute | solution.py:235
  15.9 14.1 %collective-permute-start.1 = (bf16[8,64,256]{2,1,0:T(8,128)(2,1)S(1)}, bf16[8,64,256]{2,1,0:T(8,128)(2,1)S(1)}, u32[]{:S(2)}, u32[]{:S(2)}) collective-permute-start(bf16[8,64,256]{2,1,0:T(8,128)(2,1)S(1)} %copy-done.2), channel_id=1, source_target_pairs={{0,16},{16,0},{32,48},{48,32},{64,80},{80,64},{96,112},{112,96},{1... | collective-permute-start | bytes 786440 | tf_op jit(solution)/shard_map/ppermute | solution.py:235
  17.5 71.9 %all-to-all-start.1 = ((bf16[16,64,512]{2,1,0:T(8,128)(2,1)}), bf16[16,64,512]{2,1,0:T(8,128)(2,1)}, u32[]{:S(2)}, u32[]{:S(2)}) async-start(bf16[16,64,512]{2,1,0:T(8,128)(2,1)} %broadcast_in_dim.192), calls=%async_computation.1 | async-start | bytes 2097152 | tf_op jit(solution)/shard_map/all_to_all | solution.py:247
  29.4 5.5 %copy-start.17 = (bf16[64,640]{1,0:T(8,128)(2,1)}, bf16[64,640]{1,0:T(8,128)(2,1)S(1)}, u32[]{:S(2)}) copy-start(bf16[64,640]{1,0:T(8,128)(2,1)S(1)} %collective-permute-done.2.message_ref) | copy-start | bytes 245764
  29.4 15.7 %collective-permute-start.8 = (bf16[64,640]{1,0:T(8,128)(2,1)S(1)}, bf16[64,640]{1,0:T(8,128)(2,1)}, u32[]{:S(2)}, u32[]{:S(2)}) collective-permute-start(bf16[64,640]{1,0:T(8,128)(2,1)S(1)} %pad_maximum_fusion.message_ref), channel_id=1, source_target_pairs={{0,128},{16,144},{32,160},{48,176},{64,192},{80,208},{96,224},{112... | collective-permute-start | bytes 245768 | tf_op jit(solution)/shard_map/ppermute | solution.py:228
  30.0 21.1 %collective-permute-start.10 = (bf16[64,640]{1,0:T(8,128)(2,1)S(1)}, bf16[64,640]{1,0:T(8,128)(2,1)}, u32[]{:S(2)}, u32[]{:S(2)}) collective-permute-start(bf16[64,640]{1,0:T(8,128)(2,1)S(1)} %pad_maximum_fusion.message_ref), channel_id=1, source_target_pairs={{0,160},{16,176},{32,192},{48,208},{64,224},{80,240},{96,0},{112,1... | collective-permute-start | bytes 245768 | tf_op jit(solution)/shard_map/ppermute | solution.py:228
  38.2 29.6 %collective-permute-start.3 = (bf16[288,256]{1,0:T(8,128)(2,1)}, bf16[288,256]{1,0:T(8,128)(2,1)S(1)}, u32[]{:S(2)}, u32[]{:S(2)}) collective-permute-start(bf16[288,256]{1,0:T(8,128)(2,1)} %shard_map.102), channel_id=1, source_target_pairs={{0,224},{16,240},{32,0},{48,16},{64,32},{80,48},{96,64},{112,80},{... | collective-permute-start | bytes 442376 | tf_op jit(solution)/shard_map/ppermute | solution.py:228
  42.3 27.3 %collective-permute-start.5 = (bf16[288,256]{1,0:T(8,128)(2,1)}, bf16[288,256]{1,0:T(8,128)(2,1)S(1)}, u32[]{:S(2)}, u32[]{:S(2)}) collective-permute-start(bf16[288,256]{1,0:T(8,128)(2,1)} %shard_map.103), channel_id=1, source_target_pairs={{0,192},{16,208},{32,224},{48,240},{64,0},{80,16},{96,32},{112,48}... | collective-permute-start | bytes 442376 | tf_op jit(solution)/shard_map/ppermute | solution.py:228
  45.0 11.8 %collective-permute-start.12 = (bf16[64,640]{1,0:T(8,128)(2,1)S(1)}, bf16[64,640]{1,0:T(8,128)(2,1)S(1)}, u32[]{:S(2)}, u32[]{:S(2)}) collective-permute-start(bf16[64,640]{1,0:T(8,128)(2,1)S(1)} %pad_maximum_fusion.message_ref), channel_id=1, source_target_pairs={{0,192},{16,208},{32,224},{48,240},{64,0},{80,16},{96,32},{112,48}... | collective-permute-start | bytes 245768 | tf_op jit(solution)/shard_map/ppermute | solution.py:228
  45.1 16.5 %collective-permute-start.14 = (bf16[64,640]{1,0:T(8,128)(2,1)S(1)}, bf16[64,640]{1,0:T(8,128)(2,1)S(1)}, u32[]{:S(2)}, u32[]{:S(2)}) collective-permute-start(bf16[64,640]{1,0:T(8,128)(2,1)S(1)} %pad_maximum_fusion.message_ref), channel_id=1, source_target_pairs={{0,224},{16,240},{32,0},{48,16},{64,32},{80,48},{96,64},{112,80},{... | collective-permute-start | bytes 245768 | tf_op jit(solution)/shard_map/ppermute | solution.py:228
  51.0 22.4 %collective-permute-start.7 = (bf16[288,256]{1,0:T(8,128)(2,1)}, bf16[288,256]{1,0:T(8,128)(2,1)S(1)}, u32[]{:S(2)}, u32[]{:S(2)}) collective-permute-start(bf16[288,256]{1,0:T(8,128)(2,1)} %shard_map.104), channel_id=1, source_target_pairs={{0,160},{16,176},{32,192},{48,208},{64,224},{80,240},{96,0},{112,1... | collective-permute-start | bytes 442376 | tf_op jit(solution)/shard_map/ppermute | solution.py:228
  56.9 14.0 %copy-start.22 = (s32[64]{0:T(128)S(1)}, s32[64]{0:T(128)}, u32[]{:S(2)}) copy-start(s32[64]{0:T(128)} %param.16) | copy-start | bytes 772
  56.9 16.5 %collective-permute-start.9 = (bf16[288,256]{1,0:T(8,128)(2,1)}, bf16[288,256]{1,0:T(8,128)(2,1)S(1)}, u32[]{:S(2)}, u32[]{:S(2)}) collective-permute-start(bf16[288,256]{1,0:T(8,128)(2,1)} %shard_map.105), channel_id=1, source_target_pairs={{0,128},{16,144},{32,160},{48,176},{64,192},{80,208},{96,224},{112... | collective-permute-start | bytes 442376 | tf_op jit(solution)/shard_map/ppermute | solution.py:228
  61.7 17.9 %collective-permute-start.11 = (bf16[288,256]{1,0:T(8,128)(2,1)}, bf16[288,256]{1,0:T(8,128)(2,1)S(1)}, u32[]{:S(2)}, u32[]{:S(2)}) collective-permute-start(bf16[288,256]{1,0:T(8,128)(2,1)} %shard_map.106), channel_id=1, source_target_pairs={{0,96},{16,112},{32,128},{48,144},{64,160},{80,176},{96,192},{112,... | collective-permute-start | bytes 442376 | tf_op jit(solution)/shard_map/ppermute | solution.py:228
  67.8 18.8 %copy-start.6 = (bf16[288,256]{1,0:T(8,128)(2,1)}, bf16[288,256]{1,0:T(8,128)(2,1)S(1)}, u32[]{:S(2)}) copy-start(bf16[288,256]{1,0:T(8,128)(2,1)S(1)} %collective-permute-done.3.refs_1_) | copy-start | bytes 442372
  67.8 16.6 %collective-permute-start.13 = (bf16[288,256]{1,0:T(8,128)(2,1)}, bf16[288,256]{1,0:T(8,128)(2,1)S(1)}, u32[]{:S(2)}, u32[]{:S(2)}) collective-permute-start(bf16[288,256]{1,0:T(8,128)(2,1)} %shard_map.107), channel_id=1, source_target_pairs={{0,64},{16,80},{32,96},{48,112},{64,128},{80,144},{96,160},{112,17... | collective-permute-start | bytes 442376 | tf_op jit(solution)/shard_map/ppermute | solution.py:228
  69.6 17.0 %copy-start.7 = (bf16[288,256]{1,0:T(8,128)(2,1)}, bf16[288,256]{1,0:T(8,128)(2,1)S(1)}, u32[]{:S(2)}) copy-start(bf16[288,256]{1,0:T(8,128)(2,1)S(1)} %collective-permute-done.5.refs_2_) | copy-start | bytes 442372
  69.6 17.0 %collective-permute-start.15 = (bf16[288,256]{1,0:T(8,128)(2,1)}, bf16[288,256]{1,0:T(8,128)(2,1)S(1)}, u32[]{:S(2)}, u32[]{:S(2)}) collective-permute-start(bf16[288,256]{1,0:T(8,128)(2,1)} %shard_map.108), channel_id=1, source_target_pairs={{0,32},{16,48},{32,64},{48,80},{64,96},{80,112},{96,128},{112,144}... | collective-permute-start | bytes 442376 | tf_op jit(solution)/shard_map/ppermute | solution.py:228
  73.4 13.2 %copy-start.8 = (bf16[288,256]{1,0:T(8,128)(2,1)}, bf16[288,256]{1,0:T(8,128)(2,1)S(1)}, u32[]{:S(2)}) copy-start(bf16[288,256]{1,0:T(8,128)(2,1)S(1)} %collective-permute-done.7.refs_3_) | copy-start | bytes 442372
  73.4 13.2 %copy-start.9 = (bf16[288,256]{1,0:T(8,128)(2,1)}, bf16[288,256]{1,0:T(8,128)(2,1)S(1)}, u32[]{:S(2)}) copy-start(bf16[288,256]{1,0:T(8,128)(2,1)S(1)} %collective-permute-done.9.refs_4_) | copy-start | bytes 442372
  79.5 7.2 %copy-start.10 = (bf16[288,256]{1,0:T(8,128)(2,1)}, bf16[288,256]{1,0:T(8,128)(2,1)S(1)}, u32[]{:S(2)}) copy-start(bf16[288,256]{1,0:T(8,128)(2,1)S(1)} %collective-permute-done.11.refs_5_) | copy-start | bytes 442372
  89.4 18.4 %all-to-all-start = ((bf16[16,32,256]{2,1,0:T(8,128)(2,1)}), bf16[16,32,256]{2,1,0:T(8,128)(2,1)S(1)}, u32[]{:S(2)}, u32[]{:S(2)}) async-start(bf16[16,32,256]{2,1,0:T(8,128)(2,1)} %shard_map.109), calls=%async_computation | async-start | bytes 524288 | tf_op jit(solution)/shard_map/all_to_all | solution.py:280
  112.5 13.5 %all-to-all-start.2 = ((bf16[16,4,256]{2,1,0:T(4,128)(2,1)}), bf16[16,4,256]{2,1,0:T(4,128)(2,1)S(1)}, u32[]{:S(2)}, u32[]{:S(2)}) async-start(bf16[16,4,256]{2,1,0:T(4,128)(2,1)} %all_to_all.20), calls=%async_computation.2 | async-start | bytes 65536 | tf_op jit(solution)/shard_map/all_to_all | solution.py:285
  (10 other events, 18.7 us)
